TPU v7x, 512 devices: a whole 4x8x8 slice. The times are simulated.
512 devices in a mesh: ctx: 128 (over x_lo, z, y), tp: 4 (over x_hi, core).
Axes of the slice: x: 4 (x_hi: 2, x_lo: 2; x = x_hi * 2 + x_lo), y: 8, z: 8, core: 2. Of those that a mesh axis runs over, the one named last changes fastest.
Arguments:
- queries: bfloat16 [16384, 4096], P('ctx', 'tp'), may hold values from -12 to 12
- key_states: bfloat16 [16384, 1024], P('ctx', 'tp'), may hold values from -30 to 30
- value_states: bfloat16 [16384, 1024], P('ctx', 'tp'), may hold values from -6 to 6
Outputs:
- attended: bfloat16 [16384, 4096], P(('ctx', 'tp'))
All inputs are finite; a program needn't handle non-finite values.
Results may differ from a plain program's by a relative error of at most 0.0049.
Values may be sent and summed in bfloat16 or wider, within the bound.
No kernel may reach another device: no remote copies, remote signals or barrier semaphores. Data moves between devices by JAX's collectives and lax.ppermute only.
A program may use at most 192 MiB of HBM per device.

v0:
```python
import jax
import jax.numpy as jnp
from jax import lax
from jax.sharding import PartitionSpec as P

HD = 128
HQ = 32
KVH = 8


SOFT_CAP = 50.0
QUERY_SCALE = 1.0 / 12.0


def position_of(stored_rows, tok_rows, half_rows, ctx_count):
    device = stored_rows // tok_rows
    within = stored_rows % tok_rows
    early = device * half_rows + within
    late = (2 * ctx_count - 1 - device) * half_rows + within - half_rows
    return jnp.where(within < half_rows, early, late)


def contribute(query_part, query_pos, key_block, value_block, key_pos):
    scores = (
        jnp.einsum("qkgd,rkd->kgqr", query_part, key_block, preferred_element_type=jnp.float32)
        * QUERY_SCALE
    )
    capped = SOFT_CAP * jnp.tanh(scores / SOFT_CAP)
    allowed = key_pos[None, :] <= query_pos[:, None]
    expd = jnp.where(allowed, jnp.exp(capped), jnp.float32(0.0))
    totals = jnp.sum(expd, axis=-1)
    mixed = jnp.einsum(
        "kgqr,rkd->qkgd", expd.astype(jnp.bfloat16), value_block, preferred_element_type=jnp.float32
    )
    return (totals, mixed)


def nothing(query_part, query_pos, key_block, value_block, key_pos):
    count_rows = query_part.shape[0]
    kv_count = key_block.shape[1]
    group_size = query_part.shape[2]
    return (
        jnp.zeros((kv_count, group_size, count_rows), jnp.float32),
        jnp.zeros((count_rows, kv_count, group_size, HD), jnp.float32),
    )


def body(queries, key_states, value_states):
    ctx_count = lax.axis_size("ctx")
    ctx_index = lax.axis_index("ctx")
    tok_rows = queries.shape[0]
    half_rows = tok_rows // 2
    kv_count = key_states.shape[1] // HD
    group_size = HQ // KVH
    query_heads = queries.shape[1] // HD
    query_pos = position_of(
        ctx_index * tok_rows + jnp.arange(tok_rows, dtype=jnp.int32), tok_rows, half_rows, ctx_count
    )
    shaped = queries.reshape(tok_rows, kv_count, group_size, HD)
    shard_part = (
        lax.all_gather(key_states, "ctx", axis=0, tiled=True),
        lax.all_gather(value_states, "ctx", axis=0, tiled=True),
    )
    stored_rows = jnp.arange(shard_part[0].shape[0], dtype=jnp.int32)
    key_pos = position_of(stored_rows, tok_rows, half_rows, ctx_count)
    key_part = shard_part[0]
    key_rows = key_part.shape[0]
    key_block = key_part.reshape(key_rows, kv_count, HD)
    value_block = shard_part[1].reshape(key_rows, kv_count, HD)
    key_ranges = ((0, key_rows // 2), (key_rows // 2, key_rows))
    total_parts = []
    mixed_parts = []
    for query_start, query_stop in ((0, half_rows), (half_rows, tok_rows)):
        query_part = shaped[query_start:query_stop]
        part_pos = query_pos[query_start:query_stop]
        total_sum, mixed_sum = nothing(query_part, part_pos, key_block, value_block, key_pos)
        for key_start, key_stop in key_ranges:
            range_pos = key_pos[key_start:key_stop]
            needed = jnp.min(range_pos) <= jnp.max(part_pos)
            total_add, mixed_add = lax.cond(
                needed,
                contribute,
                nothing,
                query_part,
                part_pos,
                key_block[key_start:key_stop],
                value_block[key_start:key_stop],
                range_pos,
            )
            total_sum = total_sum + total_add
            mixed_sum = mixed_sum + mixed_add
        total_parts.append(total_sum)
        mixed_parts.append(mixed_sum)
    totals = jnp.concatenate(total_parts, axis=2)
    mixed = jnp.concatenate(mixed_parts, axis=0)
    running = (totals, mixed)
    totals, mixed = running
    result = mixed / jnp.transpose(totals, (2, 0, 1))[..., None]
    finished = result.reshape(tok_rows, query_heads * HD).astype(jnp.bfloat16)
    return lax.all_to_all(finished, "tp", split_axis=0, concat_axis=1, tiled=True)


def solution(mesh):
    placed = (P("ctx", "tp"), P("ctx", "tp"), P("ctx", "tp"))
    return jax.shard_map(
        body, mesh=mesh, in_specs=placed, out_specs=P(("ctx", "tp"), None), check_vma=False
    )
```

profile of v0, /device:TPU:1, one launch (start us, length us, event | category | flops | bytes accessed | tf_op | source)
XLA Modules:
  0.0 1039.9 jit_solution(2778979051676610297)
XLA Ops:
  6.5 1.6 copy.22
  8.2 1.6 copy.23
  9.8 0.7 slice_reduce_fusion.1
  10.6 0.7 slice_reduce_fusion.2
  16.4 1.0 fusion.61
  17.5 413.8 %all-gather.3.cloned.1.call-done = bf16[16384,256]{0,1:T(8,128)(2,1)} async-done(((bf16[128,256]{0,1:T(8,128)(2,1)}), bf16[16384,256]{0,1:T(8,128)(2,1)}) %all-gather.3.cloned.1.call-update) | async-done | bytes 8388624 | tf_op jit(solution)/shard_map/all_gather | solution.py:61
  431.3 5.9 fusion.60
  437.2 473.1 %all-gather.5.cloned.1.call-done = bf16[16384,256]{0,1:T(8,128)(2,1)} async-done(((bf16[128,256]{0,1:T(8,128)(2,1)}), bf16[16384,256]{0,1:T(8,128)(2,1)}) %all-gather.5.cloned.1.call-update) | async-done | bytes 8388624 | tf_op jit(solution)/shard_map/all_gather | solution.py:62
  910.3 6.6 fusion.59
  916.9 0.3 copy-done.2
  917.1 10.9 %conditional.6 = (f32[2,4,64]{2,1,0:T(4,128)S(1)}, f32[64,2,4,128]{3,0,2,1:T(8,128)S(1)}) conditional(s32[]{:T(128)} %convert_element_type.30, () %tuple.41, (s32[8192]{0:T(1024)S(1)}, s32[64]{0:T(128)S(1)}, bf16[8192,2,128]{0,2,1:T(8,128)(2,1)S(1)}, bf16[64,2,4,128]{3,2,1,0:T(4,128)(2,1)S(1)}, bf16[8192,2,128]{0,2,1:T(8,128)(2,1)}) %tuple.87), branch_computations={%region_10.11_spmd, %region_11.13_spmd} | conditional | flops 2168978944 | bytes 26642704 | solution.py:80
  917.1 0.3 broadcast_compare_fusion.2
  917.5 6.0 fusion.57
  923.5 4.5 fusion.24
  928.0 11.9 %conditional.7 = (f32[2,4,64]{2,1,0:T(4,128)S(1)}, f32[64,2,4,128]{3,0,2,1:T(8,128)S(1)}) conditional(s32[]{:T(128)} %convert_element_type.31, () %tuple.43, (s32[8192]{0:T(1024)S(1)}, s32[64]{0:T(128)S(1)}, bf16[8192,2,128]{0,2,1:T(8,128)(2,1)}, bf16[64,2,4,128]{3,2,1,0:T(4,128)(2,1)S(1)}, bf16[8192,2,128]{0,2,1:T(8,128)(2,1)}) %tuple.84), branch_computations={%region_13.14_spmd, %region_14.16_spmd} | conditional | flops 2168978944 | bytes 43419948 | solution.py:80
  928.0 0.3 broadcast_compare_fusion.3
  928.4 9.0 fusion.58
  937.4 2.3 fusion.34
  939.9 0.2 copy.37
  940.1 0.1 concatenate.14
  940.2 13.7 %conditional.4 = (f32[2,4,64]{2,1,0:T(4,128)S(1)}, f32[64,2,4,128]{3,0,2,1:T(8,128)S(1)}) conditional(s32[]{:T(128)} %convert_element_type.28, () %tuple.37, (s32[8192]{0:T(1024)S(1)}, s32[64]{0:T(128)S(1)}, bf16[8192,2,128]{0,2,1:T(8,128)(2,1)}, bf16[64,2,4,128]{3,2,1,0:T(4,128)(2,1)S(1)}, bf16[8192,2,128]{0,2,1:T(8,128)(2,1)}) %tuple.86), branch_computations={%region_2.3_spmd, %region_3.5_spmd} | conditional | flops 2168978944 | bytes 26642704 | solution.py:80
  940.2 0.3 broadcast_compare_fusion
  940.6 8.8 fusion.55
  949.4 4.5 fusion.4
  954.0 0.2 copy.30
  954.2 0.1 concatenate.13
  954.4 0.2 copy.38
  954.6 0.3 div.68
  954.9 0.2 div.69
  955.2 0.1 divide_convert_fusion
  955.3 77.0 %all_to_all.16 = bf16[4,32,1024]{2,1,0:T(8,128)(2,1)S(1)} all-to-all(bf16[4,32,1024]{2,1,0:T(8,128)(2,1)S(1)} %divide_convert_fusion), channel_id=1, replica_groups=mesh['ctx'=128,'tp'=4] {'tp'}, dimensions={0} | all-to-all | bytes 524288 | tf_op jit(solution)/shard_map/all_to_all | solution.py:100
  1032.3 0.7 copy.64
  (20 shorter events, 0.5 us)
Async XLA Ops:
  6.5 424.8 %all-gather.3.cloned.1.call-start = ((), (), s32[]{:S(2)}) async-start(), calls=%async_computation.1 | async-start | bytes 8454144 | tf_op jit(solution)/shard_map/all_gather | solution.py:61
  8.1 902.2 %all-gather.5.cloned.1.call-start = ((), (), s32[]{:S(2)}) async-start(), calls=%async_computation.2 | async-start | bytes 8454144 | tf_op jit(solution)/shard_map/all_gather | solution.py:62
  910.3 6.8 copy-start.2
  928.4 9.0 copy-start
Sparse Core Ops, SparseCore 0:
  9.4 421.9 all-gather.2
  433.3 476.9 all-gather.4
where the time goes:
time: 1050 us; the launch traced here: 1040 us
  waiting for transfers between devices  887 us (84%)
  blocking collectives  77 us (7%)
  matrix products  35.1 us (3%)
  local copies, waits for them, and re-layouts  19 us (2%)
  between operations  18.7 us (2%)
    all_gather x1, waiting for transfers between devices, body(): lax.all_gather(value_states, 'ctx', axis=0, tiled=True)  473 us
    all_gather x1, waiting for transfers between devices, body(): lax.all_gather(key_states, 'ctx', axis=0, tiled=True)  414 us
    all_to_all x1, blocking collectives, body(): lax.all_to_all(finished, 'tp', split_axis=0, concat_axis=1, tiled=True)  77 us
    dot_general x3, matrix products, contribute(): jnp.einsum('qkgd,rkd->kgqr', query_part, key_block, preferred_element_typ...  23.8 us
  transfers between devices with their start and end apart: 2, of which 2 were waited for; matrix products, arithmetic and copies ran while one was open for 1% of the time, Pallas kernels for 0%

commit v1 on v0

v1 whole, which is shorter than its diff:
```python
import functools
import math

import jax
import jax.numpy as jnp
from jax import lax
from jax.experimental import pallas as pl
from jax.experimental.pallas import tpu as pltpu
from jax.sharding import Mesh, PartitionSpec as P

AXES = ("xl", "zh", "zm", "zl", "yh", "ym", "yl", "xh", "co")
CTX = AXES[:7]
TP = AXES[7:]
QUERY_GROUP = ("zh", "zm", "yh")
KEY_GROUP = ("xl", "zl", "ym", "yl")

HD = 128
GROUP = 4
WIDE = GROUP * HD
RANGE = 512
RANGES = 32
ARG_SCALE = 1.0 / 600.0
EXP_SCALE = 50.0 * math.log2(math.e)
STEP = 2

bf16 = jnp.bfloat16
f32 = jnp.float32


def attend_kernel(place_ref, q_ref, kv0_ref, kv1_ref, out_ref, q_scr, acc_scr, sum_scr):
    base, w_own, core, part = place_ref[0], place_ref[1], place_ref[2], place_ref[3]
    rows = GROUP * 64

    def tile_of(ref, which, t):
        late = (t >= RANGES // 2).astype(jnp.int32)
        m = jnp.where(late == 1, RANGES - 1 - t, t)
        x = (m // 8) * 2 + m % 2
        zz = (m // 2) % 4
        return ref[x, :, which, zz, :, late].reshape(128, HD)

    def tiles(which, t0):
        parts = []
        for i in range(STEP):
            parts += [tile_of(kv0_ref, which, t0 + i), tile_of(kv1_ref, which, t0 + i)]
        return jnp.concatenate(parts, axis=0)

    def chunk(k, _):
        zz, e = k % 4, k // 4
        for g in range(GROUP):
            q_scr[g * 64 : (g + 1) * 64, :] = q_ref[zz, :, e, :, g * HD : (g + 1) * HD].reshape(64, HD)
        m_early = base + 2 * zz
        m = jnp.where(e == 1, RANGES - 1 - m_early, m_early)
        acc_scr[...] = jnp.zeros_like(acc_scr)
        sum_scr[...] = jnp.zeros_like(sum_scr)

        def step(t0, masked):
            s = lax.dot_general(
                q_scr[...], tiles(0, t0), (((1,), (1,)), ((), ())), preferred_element_type=f32
            )
            w = jnp.exp2(jnp.tanh(s * ARG_SCALE) * EXP_SCALE)
            if masked:
                n = lax.broadcasted_iota(jnp.int32, w.shape, 1)
                r = lax.broadcasted_iota(jnp.int32, w.shape, 0)
                t = t0 + n // 256
                other = (n // 128) % 2
                n8 = ((n // 16) % 2) * 4 + (n // 32) % 4
                n8 = jnp.where(t >= RANGES // 2, 7 - n8, n8)
                key_core = jnp.where(other == 1, 1 - core, core)
                key_pos = t * RANGE + n8 * 64 + key_core * 32 + part * 16 + n % 16
                r8 = ((r // 32) % 2) * 4 + w_own
                r8 = jnp.where(e == 1, 7 - r8, r8)
                query_pos = m * RANGE + r8 * 64 + core * 32 + r % 32
                w = jnp.where(key_pos <= query_pos, w, 0.0)
            total = w[:, 0:HD]
            for i in range(1, w.shape[1] // HD):
                total = total + w[:, i * HD : (i + 1) * HD]
            sum_scr[...] += total
            acc_scr[...] += jnp.dot(w.astype(bf16), tiles(1, t0), preferred_element_type=f32)

        def full(i, c):
            step(i * STEP, False)
            return c

        lax.fori_loop(0, m // STEP, full, 0)
        step((m // STEP) * STEP, True)

        lane = lax.broadcasted_iota(jnp.int32, (64, HD), 1) // 16
        packed = jnp.zeros((64, HD), f32)
        for g in range(GROUP):
            piece = slice(g * 64, (g + 1) * 64)
            out_ref[zz, :, e, :, g * HD : (g + 1) * HD] = (
                acc_scr[piece, :].astype(bf16).reshape(2, 32, HD)
            )
            total = jnp.sum(sum_scr[piece, :], axis=1, keepdims=True)
            high = total.astype(bf16).astype(f32)
            packed = jnp.where(lane == 2 * g, high, packed)
            packed = jnp.where(lane == 2 * g + 1, total - high, packed)
        out_ref[zz, :, e, :, WIDE:] = packed.astype(bf16).reshape(2, 32, HD)
        return 0

    lax.fori_loop(0, 8, chunk, 0)


def attend(place, q, kv0, kv1):
    vmem = pl.BlockSpec(memory_space=pltpu.VMEM)
    return pl.pallas_call(
        attend_kernel,
        out_shape=jax.ShapeDtypeStruct(q.shape, bf16),
        in_specs=[pl.BlockSpec(memory_space=pltpu.SMEM), vmem, vmem, vmem],
        out_specs=vmem,
        scratch_shapes=[
            pltpu.VMEM((GROUP * 64, HD), bf16),
            pltpu.VMEM((GROUP * 64, HD), f32),
            pltpu.VMEM((GROUP * 64, HD), f32),
        ],
        compiler_params=pltpu.CompilerParams(vmem_limit_bytes=48 * 1024 * 1024),
        name="attend",
    )(place, q, kv0, kv1)


def finish_kernel(x_ref, out_ref):
    for xh in range(2):
        for zz in range(4):
            totals = x_ref[zz, 0, xh, :, WIDE:].astype(f32) + x_ref[zz, 1, xh, :, WIDE:].astype(f32)
            for g in range(GROUP):
                cols = slice(g * HD, (g + 1) * HD)
                mixed = x_ref[zz, 0, xh, :, cols].astype(f32) + x_ref[zz, 1, xh, :, cols].astype(f32)
                at = 32 * g
                total = totals[:, at : at + 1] + totals[:, at + 16 : at + 17]
                first = (xh * 4 + zz) * WIDE + g * HD
                out_ref[:, first : first + HD] = (mixed / total).astype(bf16)


def finish(x):
    vmem = pl.BlockSpec(memory_space=pltpu.VMEM)
    return pl.pallas_call(
        finish_kernel,
        out_shape=jax.ShapeDtypeStruct((32, 8 * WIDE), bf16),
        in_specs=[vmem],
        out_specs=vmem,
        name="finish",
    )(x)


def body(queries, keys, values):
    with jax.named_scope("to_cores"):
        mine = jnp.concatenate([queries, keys, values], axis=1).reshape(2, 2, 32, 1536)
        mine = mine.transpose(1, 0, 2, 3).reshape(2, 64, 1536)
        heads = lax.all_to_all(mine, "co", 0, 0)
    with jax.named_scope("to_heads"):
        q = heads[:, :, :1024].reshape(2, 64, 2, WIDE).transpose(0, 2, 1, 3)
        kv = heads[:, :, 1024:].reshape(2, 2, 2, 16, 2, 2, HD)
        kv = kv.transpose(0, 5, 2, 4, 1, 3, 6).reshape(2, 2, 2, 64, HD)
        q = jnp.broadcast_to(q[:, :, None], (2, 2, 2, 64, WIDE))
        sent = jnp.concatenate([q, kv], axis=-1).reshape(8, 64, WIDE + HD)
        got = lax.all_to_all(sent, QUERY_GROUP, 0, 0)
    with jax.named_scope("keys_values"):
        kv = got[:, :, WIDE:].reshape(8, 2, 2, 16, HD).transpose(1, 0, 2, 3, 4)
        spread = jnp.broadcast_to(kv[None], (16,) + kv.shape).reshape(16, -1, HD)
        kv0 = lax.all_to_all(spread, KEY_GROUP, 0, 0)
        kv1 = lax.ppermute(kv0, "co", [(0, 1), (1, 0)])
    at = {a: lax.axis_index(a) for a in AXES}
    place = jnp.stack(
        [at["xl"] * 8 + at["zl"], at["ym"] * 2 + at["yl"], at["co"], at["yh"]]
    ).astype(jnp.int32)
    shape = (4, 4, 2, 4, 2, 2, 16, HD)
    mixed = attend(place, got.reshape(4, 2, 2, 32, WIDE + HD), kv0.reshape(shape), kv1.reshape(shape))
    with jax.named_scope("to_owners"):
        owned = lax.all_to_all(mixed.reshape(16, 32, WIDE + HD), QUERY_GROUP + ("xh",), 0, 0)
    return finish(owned.reshape(4, 2, 2, 32, WIDE + HD))


def solution(mesh):
    fine = Mesh(mesh.devices.reshape((2,) * len(AXES)), AXES)
    return jax.shard_map(
        body, mesh=fine, in_specs=P(CTX, TP), out_specs=P(CTX + TP, None), check_vma=False
    )
```

time: 1050 us -> 170 us (0.16)
  waiting for transfers between devices: 887 us -> 3.81 us
  blocking collectives: 77 us -> 125 us
  matrix products: 35.1 us -> 0 us
  Pallas kernels: 0 us -> 34.2 us
  between operations: 18.7 us -> 0.12 us
  local copies, waits for them, and re-layouts: 19 us -> 0.8 us
    all_gather x2 -> x0, waiting for transfers between devices: 887 us -> none  [the longest x1 473 us: body(): lax.all_gather(value_states, 'ctx', axis=0, tiled=True)]
    all_to_all x1 -> x4, blocking collectives: 77 us -> 125 us  [the longest x1 58.5 us: body(): kv0 = lax.all_to_all(spread, KEY_GROUP, 0, 0)]
    dot_general x6 -> x0, matrix products: 35.1 us -> none  [the longest x3 23.8 us: contribute(): jnp.einsum('qkgd,rkd->kgqr', query_part, key_block, preferred_element_typ...]
    pallas_call x0 -> x2, Pallas kernels: none -> 34.2 us  [the longest x1 31.8 us: attend(): pl.pallas_call(attend_kernel, out_shape=jax.ShapeDtypeStruct(q.shape, bf1...]
    slice x5 -> x3, local copies, waits for them, and re-layouts: 13.6 us -> 0.05 us  [the longest x1 0.02 us: body(): kv = got[:, :, WIDE:].reshape(8, 2, 2, 16, HD).transpose(1, 0, 2, 3, 4)]
  transfers between devices with their start and end apart: 2 -> 1, of which waited for: 2 -> 1; matrix products, arithmetic and copies ran while one was open for 1% -> 0% of each run, Pallas kernels for 0% -> 0%
where the time goes in v1:
time: 170 us; the launch traced here: 169 us
  blocking collectives  125 us (74%)
  Pallas kernels  34.2 us (20%)
  waiting for transfers between devices  3.81 us (2%)
  starting transfers between devices  3.65 us (2%)
    all_to_all x1, blocking collectives, body(): kv0 = lax.all_to_all(spread, KEY_GROUP, 0, 0)  58.5 us
    pallas_call x1, Pallas kernels, attend(): pl.pallas_call(attend_kernel, out_shape=jax.ShapeDtypeStruct(q.shape, bf1...  31.8 us
    all_to_all x1, blocking collectives, body(): got = lax.all_to_all(sent, QUERY_GROUP, 0, 0)  28.6 us
    all_to_all x1, blocking collectives, body(): lax.all_to_all(mixed.reshape(16, 32, WIDE + HD), QUERY_GROUP + ('xh',), 0...  27.7 us
    all_to_all x1, blocking collectives, body(): heads = lax.all_to_all(mine, 'co', 0, 0)  10.6 us
    ppermute x1, waiting for transfers between devices, body(): kv1 = lax.ppermute(kv0, 'co', [(0, 1), (1, 0)])  3.81 us
    ppermute x1, starting transfers between devices, body(): kv1 = lax.ppermute(kv0, 'co', [(0, 1), (1, 0)])  3.65 us
  transfers between devices with their start and end apart: 1, of which 1 were waited for; matrix products, arithmetic and copies ran while one was open for 0% of the time, Pallas kernels for 0%

profile of v1, /device:TPU:1, one launch (start us, length us, event | category | flops | bytes accessed | tf_op | source)
XLA Modules:
  0.0 169.1 jit_solution(4320583455048580831)
XLA Ops:
  0.0 1.1 pad_maximum_fusion.1
  1.1 10.6 %all_to_all.20 = bf16[2,64,1536]{2,1,0:T(8,128)(2,1)S(1)} all-to-all(bf16[2,64,1536]{2,1,0:T(8,128)(2,1)S(1)} %bitcast.26), channel_id=1, replica_groups=mesh['xl'=2,'zh'=2,'zm'=2,'zl'=2,'yh'=2,'ym'=2,'yl'=2,'xh'=2,'co'=2] {'co'}, dimensions={0} | all-to-all | bytes 786432 | tf_op jit(solution)/shard_map/to_cores/all_to_all | solution.py:149
  11.7 0.2 reshape.42
  12.0 0.1 pad_maximum_fusion
  12.1 28.6 %all_to_all.21 = bf16[8,64,640]{2,1,0:T(8,128)(2,1)S(1)} all-to-all(bf16[8,64,640]{2,1,0:T(8,128)(2,1)S(1)} %pad_maximum_fusion), channel_id=1, replica_groups=mesh['xl'=2,'zh'=2,'zm'=2,'zl'=2,'yh'=2,'ym'=2,'yl'=2,'xh'=2,'co'=2] {'z..., dimensions={0} | all-to-all | bytes 1310720 | tf_op jit(solution)/shard_map/to_heads/all_to_all | solution.py:156
  40.7 0.4 broadcast_in_dim.16
  41.1 58.5 %all_to_all.22 = bf16[16,512,128]{2,1,0:T(8,128)(2,1)S(1)} all-to-all(bf16[16,512,128]{2,1,0:T(8,128)(2,1)S(1)} %broadcast_in_dim.16), channel_id=1, replica_groups=mesh['xl'=2,'zh'=2,'zm'=2,'zl'=2,'yh'=2,'ym'=2,'yl'=2,'xh'=2,'co'=2] {'x..., dimensions={0} | all-to-all | bytes 4194304 | tf_op jit(solution)/shard_map/keys_values/all_to_all | solution.py:160
  99.6 3.7 %collective-permute-start = (bf16[16,512,128]{2,1,0:T(8,128)(2,1)S(1)}, bf16[16,512,128]{2,1,0:T(8,128)(2,1)}, u32[]{:S(2)}, u32[]{:S(2)}) collective-permute-start(bf16[16,512,128]{2,1,0:T(8,128)(2,1)S(1)} %all_to_all.22), channel_id=1, source_target_pairs={{0,1},{1,0},{2,3},{3,2},{4,5},{5,4},{6,7},{7,6},{8,9},{9,8},{10,11... | collective-permute-start | bytes 6291464 | tf_op jit(solution)/shard_map/keys_values/ppermute | solution.py:161
  103.3 0.1 pad_add_fusion.place_ref
  103.4 3.8 %collective-permute-done = bf16[16,512,128]{2,1,0:T(8,128)(2,1)} collective-permute-done((bf16[16,512,128]{2,1,0:T(8,128)(2,1)S(1)}, bf16[16,512,128]{2,1,0:T(8,128)(2,1)}, u32[]{:S(2)}, u32[]{:S(2)}) %collective-permute-start) | collective-permute-done | bytes 2097184 | tf_op jit(solution)/shard_map/keys_values/ppermute | solution.py:161
  107.2 31.8 %attend.1 = bf16[4,2,2,32,640]{4,3,2,1,0:T(8,128)(2,1)S(1)} custom-call(s32[4]{0:T(128)S(1)} %pad_add_fusion.place_ref, bf16[4,2,2,32,640]{4,3,2,1,0:T(8,128)(2,1)S(1)} %bitcast.22, bf16[4,4,2,4,2,2,16,128]{7,6,5,4,3,2,1,0:T(8,128)(2,1)S(1)} %bitcast.21, bf16[4,4,2,4,2,2,16,128]{7,6,5,4,3,2,1,0:T(8,128)(2,1)} %bitcast.16.kv1_ref), custom_call_target="tpu_custom_call" | custom-call | tf_op jit(solution)/shard_map/attend/pallas_call | solution.py:106
  138.9 27.7 %all_to_all.23 = bf16[16,32,640]{2,1,0:T(8,128)(2,1)} all-to-all(bf16[16,32,640]{2,1,0:T(8,128)(2,1)S(1)} %bitcast.23), channel_id=1, replica_groups=mesh['xl'=2,'zh'=2,'zm'=2,'zl'=2,'yh'=2,'ym'=2,'yl'=2,'xh'=2,'co'=2] {'z..., dimensions={0} | all-to-all | bytes 1310720 | tf_op jit(solution)/shard_map/to_owners/all_to_all | solution.py:169
  166.6 2.4 %finish.1 = bf16[32,4096]{1,0:T(8,128)(2,1)} custom-call(bf16[4,2,2,32,640]{4,3,2,1,0:T(8,128)(2,1)} %bitcast.24), custom_call_target="tpu_custom_call" | custom-call | tf_op jit(solution)/shard_map/finish/pallas_call | solution.py:136
  (9 shorter events, 0.2 us)
Async XLA Ops:
  99.6 7.6 %collective-permute-start = (bf16[16,512,128]{2,1,0:T(8,128)(2,1)S(1)}, bf16[16,512,128]{2,1,0:T(8,128)(2,1)}, u32[]{:S(2)}, u32[]{:S(2)}) collective-permute-start(bf16[16,512,128]{2,1,0:T(8,128)(2,1)S(1)} %all_to_all.22), channel_id=1, source_target_pairs={{0,1},{1,0},{2,3},{3,2},{4,5},{5,4},{6,7},{7,6},{8,9},{9,8},{10,11... | collective-permute-start | bytes 6291464 | tf_op jit(solution)/shard_map/keys_values/ppermute | solution.py:161

commit v2 on v1

v2 whole, which is shorter than its diff:
```python
import functools
import math

import jax
import jax.numpy as jnp
from jax import lax
from jax.experimental import pallas as pl
from jax.experimental.pallas import tpu as pltpu
from jax.sharding import Mesh, PartitionSpec as P

AXES = ("xl", "zh", "zm", "zl", "yh", "ym", "yl", "xh", "co")
CTX = AXES[:7]
TP = AXES[7:]
QUERY_GROUP = ("xl", "zl", "yl")
KEY_GROUP = ("zh", "zm", "yh", "ym")

HD = 128
GROUP = 4
WIDE = GROUP * HD
RANGE = 512
RANGES = 32
ARG_SCALE = 1.0 / 600.0
EXP_SCALE = 50.0 * math.log2(math.e)
STEP = 8
ROWS = 512

bf16 = jnp.bfloat16
f32 = jnp.float32


def attend_kernel(place_ref, q_ref, kv0_ref, kv1_ref, out_ref, q_scr, acc_scr, sum_scr):
    base, w_own, core, part = place_ref[0], place_ref[1], place_ref[2], place_ref[3]

    def tile_of(ref, which, t):
        late = (t >= RANGES // 2).astype(jnp.int32)
        m = jnp.where(late == 1, RANGES - 1 - t, t)
        x = (m // 2) % 4
        zz = (m // 8) * 2 + m % 2
        return ref[x, :, which, zz, :, late].reshape(128, HD)

    def tiles(which, t):
        return jnp.concatenate([tile_of(kv0_ref, which, t), tile_of(kv1_ref, which, t)], axis=0)

    def key_position(t):
        n = lax.broadcasted_iota(jnp.int32, (1, 256), 1)
        n8 = (n // 16) % 8
        n8 = jnp.where(t >= RANGES // 2, 7 - n8, n8)
        key_core = jnp.where(n >= 128, 1 - core, core)
        return t * RANGE + n8 * 64 + key_core * 32 + part * 16 + n % 16

    def chunk(k, _):
        xl, e = k % 2, k // 2
        for g in range(GROUP):
            q_scr[g * 128 : (g + 1) * 128, :] = q_ref[
                pl.ds(xl * 2, 2), :, e, :, g * HD : (g + 1) * HD
            ].reshape(128, HD)
        first = base + xl * 8
        first = jnp.where(e == 1, RANGES - 2 - first, first)
        acc_scr[...] = jnp.zeros_like(acc_scr)
        sum_scr[...] = jnp.zeros_like(sum_scr)

        def scores(t):
            return lax.dot_general(
                q_scr[...], tiles(0, t), (((1,), (1,)), ((), ())), preferred_element_type=f32
            )

        def run(t0, count, masked):
            ahead = scores(t0)
            acc, total = acc_scr[...], sum_scr[...]
            for t in range(count):
                s = ahead
                if t + 1 < count:
                    ahead = scores(t0 + t + 1)
                w = jnp.exp2(jnp.tanh(s * ARG_SCALE) * EXP_SCALE)
                if masked:
                    r = lax.broadcasted_iota(jnp.int32, (ROWS, 1), 0)
                    r16 = ((r // 64) % 2) * 8 + w_own * 2 + (r // 32) % 2
                    r16 = jnp.where(e == 1, 15 - r16, r16)
                    query_pos = first * RANGE + r16 * 64 + core * 32 + r % 32
                    w = jnp.where(key_position(t0 + t) <= query_pos, w, 0.0)
                total = total + (w[:, :HD] + w[:, HD:])
                acc = acc + jnp.dot(w.astype(bf16), tiles(1, t0 + t), preferred_element_type=f32)
            acc_scr[...] = acc
            sum_scr[...] = total

        def long(i, c):
            run(i * STEP, STEP, False)
            return c

        def short(i, c):
            run(first // STEP * STEP + i * 2, 2, False)
            return c

        lax.fori_loop(0, first // STEP, long, 0)
        lax.fori_loop(0, first % STEP // 2, short, 0)
        run(first, 2, True)

        lane = lax.broadcasted_iota(jnp.int32, (128, HD), 1) // 16
        packed = jnp.zeros((128, HD), f32)
        for g in range(GROUP):
            piece = slice(g * 128, (g + 1) * 128)
            out_ref[pl.ds(xl * 2, 2), :, e, :, g * HD : (g + 1) * HD] = (
                acc_scr[piece, :].astype(bf16).reshape(2, 2, 32, HD)
            )
            total = jnp.sum(sum_scr[piece, :], axis=1, keepdims=True)
            high = total.astype(bf16).astype(f32)
            packed = jnp.where(lane == 2 * g, high, packed)
            packed = jnp.where(lane == 2 * g + 1, total - high, packed)
        out_ref[pl.ds(xl * 2, 2), :, e, :, WIDE:] = packed.astype(bf16).reshape(2, 2, 32, HD)
        return 0

    lax.fori_loop(0, 4, chunk, 0)


def attend(place, q, kv0, kv1):
    vmem = pl.BlockSpec(memory_space=pltpu.VMEM)
    return pl.pallas_call(
        attend_kernel,
        out_shape=jax.ShapeDtypeStruct(q.shape, bf16),
        in_specs=[pl.BlockSpec(memory_space=pltpu.SMEM), vmem, vmem, vmem],
        out_specs=vmem,
        scratch_shapes=[
            pltpu.VMEM((ROWS, HD), bf16),
            pltpu.VMEM((ROWS, HD), f32),
            pltpu.VMEM((ROWS, HD), f32),
        ],
        compiler_params=pltpu.CompilerParams(vmem_limit_bytes=48 * 1024 * 1024),
        name="attend",
    )(place, q, kv0, kv1)


def finish_kernel(x_ref, out_ref):
    for xh in range(2):
        for zz in range(4):
            totals = x_ref[zz, 0, xh, :, WIDE:].astype(f32) + x_ref[zz, 1, xh, :, WIDE:].astype(f32)
            for g in range(GROUP):
                cols = slice(g * HD, (g + 1) * HD)
                mixed = x_ref[zz, 0, xh, :, cols].astype(f32) + x_ref[zz, 1, xh, :, cols].astype(f32)
                at = 32 * g
                total = totals[:, at : at + 1] + totals[:, at + 16 : at + 17]
                first = (xh * 4 + zz) * WIDE + g * HD
                out_ref[:, first : first + HD] = (mixed / total).astype(bf16)


def finish(x):
    vmem = pl.BlockSpec(memory_space=pltpu.VMEM)
    return pl.pallas_call(
        finish_kernel,
        out_shape=jax.ShapeDtypeStruct((32, 8 * WIDE), bf16),
        in_specs=[vmem],
        out_specs=vmem,
        name="finish",
    )(x)


def body(queries, keys, values):
    with jax.named_scope("to_cores"):
        mine = jnp.concatenate([queries, keys, values], axis=1).reshape(2, 2, 32, 1536)
        mine = mine.transpose(1, 0, 2, 3).reshape(2, 64, 1536)
        heads = lax.all_to_all(mine, "co", 0, 0)
    with jax.named_scope("to_heads"):
        q = heads[:, :, :1024].reshape(2, 64, 2, WIDE).transpose(0, 2, 1, 3)
        kv = heads[:, :, 1024:].reshape(2, 2, 2, 16, 2, 2, HD)
        kv = kv.transpose(0, 5, 2, 4, 1, 3, 6).reshape(2, 2, 2, 64, HD)
        q = jnp.broadcast_to(q[:, :, None], (2, 2, 2, 64, WIDE))
        sent = jnp.concatenate([q, kv], axis=-1).reshape(8, 64, WIDE + HD)
        got = lax.all_to_all(sent, QUERY_GROUP, 0, 0)
    with jax.named_scope("keys_values"):
        kv = got[:, :, WIDE:].reshape(8, 2, 2, 16, HD).transpose(1, 0, 2, 3, 4)
        spread = jnp.broadcast_to(kv[None], (16,) + kv.shape).reshape(16, -1, HD)
        kv0 = lax.all_to_all(spread, KEY_GROUP, 0, 0)
        kv1 = lax.ppermute(kv0, "co", [(0, 1), (1, 0)])
    at = {a: lax.axis_index(a) for a in AXES}
    place = jnp.stack(
        [at["zh"] * 4 + at["zm"] * 2, at["yh"] * 2 + at["ym"], at["co"], at["yl"]]
    ).astype(jnp.int32)
    shape = (4, 4, 2, 4, 2, 2, 16, HD)
    mixed = attend(place, got.reshape(4, 2, 2, 32, WIDE + HD), kv0.reshape(shape), kv1.reshape(shape))
    with jax.named_scope("to_owners"):
        owned = lax.all_to_all(mixed.reshape(16, 32, WIDE + HD), QUERY_GROUP + ("xh",), 0, 0)
    return finish(owned.reshape(4, 2, 2, 32, WIDE + HD))


def solution(mesh):
    fine = Mesh(mesh.devices.reshape((2,) * len(AXES)), AXES)
    return jax.shard_map(
        body, mesh=fine, in_specs=P(CTX, TP), out_specs=P(CTX + TP, None), check_vma=False
    )
```

time: 170 us -> 131 us (0.77)
  blocking collectives: 125 us -> 102 us
  Pallas kernels: 34.2 us -> 18.5 us
    pallas_call x1, Pallas kernels: 31.8 us -> 16.1 us  [attend(): pl.pallas_call(attend_kernel, out_shape=jax.ShapeDtypeStruct(q.shape, bf1...]
    all_to_all x1, blocking collectives: 28.6 us -> 13.3 us  [body(): got = lax.all_to_all(sent, QUERY_GROUP, 0, 0)]
    all_to_all x1, blocking collectives: 27.7 us -> 15.7 us  [body(): lax.all_to_all(mixed.reshape(16, 32, WIDE + HD), QUERY_GROUP + ('xh',), 0...]
    all_to_all x1, blocking collectives: 58.5 us -> 62.5 us  [body(): kv0 = lax.all_to_all(spread, KEY_GROUP, 0, 0)]
where the time goes in v2:
time: 131 us
  blocking collectives  102 us (78%)
  Pallas kernels  18.5 us (14%)
  starting transfers between devices  4.38 us (3%)
  waiting for transfers between devices  3.81 us (3%)
    all_to_all x1, blocking collectives, body(): kv0 = lax.all_to_all(spread, KEY_GROUP, 0, 0)  62.5 us
    pallas_call x1, Pallas kernels, attend(): pl.pallas_call(attend_kernel, out_shape=jax.ShapeDtypeStruct(q.shape, bf1...  16.1 us
    all_to_all x1, blocking collectives, body(): lax.all_to_all(mixed.reshape(16, 32, WIDE + HD), QUERY_GROUP + ('xh',), 0...  15.7 us
    all_to_all x1, blocking collectives, body(): got = lax.all_to_all(sent, QUERY_GROUP, 0, 0)  13.3 us
    all_to_all x1, blocking collectives, body(): heads = lax.all_to_all(mine, 'co', 0, 0)  10.6 us
    ppermute x1, starting transfers between devices, body(): kv1 = lax.ppermute(kv0, 'co', [(0, 1), (1, 0)])  4.38 us
    ppermute x1, waiting for transfers between devices, body(): kv1 = lax.ppermute(kv0, 'co', [(0, 1), (1, 0)])  3.81 us
  transfers between devices with their start and end apart: 1, of which 1 were waited for; matrix products, arithmetic and copies ran while one was open for 0% of the time, Pallas kernels for 0%

profile of v2, /device:TPU:1, one launch (start us, length us, event | category | flops | bytes accessed | tf_op | source)
XLA Modules:
  0.0 130.9 jit_solution(1888707108421978955)
XLA Ops:
  0.0 1.1 pad_maximum_fusion.1
  1.1 10.6 %all_to_all.20 = bf16[2,64,1536]{2,1,0:T(8,128)(2,1)S(1)} all-to-all(bf16[2,64,1536]{2,1,0:T(8,128)(2,1)S(1)} %bitcast.26), channel_id=1, replica_groups=mesh['xl'=2,'zh'=2,'zm'=2,'zl'=2,'yh'=2,'ym'=2,'yl'=2,'xh'=2,'co'=2] {'co'}, dimensions={0} | all-to-all | bytes 786432 | tf_op jit(solution)/shard_map/to_cores/all_to_all | solution.py:160
  11.7 0.2 reshape.42
  12.0 0.1 pad_maximum_fusion
  12.1 13.3 %all_to_all.21 = bf16[8,64,640]{2,1,0:T(8,128)(2,1)S(1)} all-to-all(bf16[8,64,640]{2,1,0:T(8,128)(2,1)S(1)} %pad_maximum_fusion), channel_id=1, replica_groups=mesh['xl'=2,'zh'=2,'zm'=2,'zl'=2,'yh'=2,'ym'=2,'yl'=2,'xh'=2,'co'=2] {'x..., dimensions={0} | all-to-all | bytes 1310720 | tf_op jit(solution)/shard_map/to_heads/all_to_all | solution.py:167
  25.5 0.4 broadcast_in_dim.16
  25.9 62.5 %all_to_all.22 = bf16[16,512,128]{2,1,0:T(8,128)(2,1)S(1)} all-to-all(bf16[16,512,128]{2,1,0:T(8,128)(2,1)S(1)} %broadcast_in_dim.16), channel_id=1, replica_groups=mesh['xl'=2,'zh'=2,'zm'=2,'zl'=2,'yh'=2,'ym'=2,'yl'=2,'xh'=2,'co'=2] {'z..., dimensions={0} | all-to-all | bytes 4194304 | tf_op jit(solution)/shard_map/keys_values/all_to_all | solution.py:171
  88.3 4.4 %collective-permute-start = (bf16[16,512,128]{2,1,0:T(8,128)(2,1)S(1)}, bf16[16,512,128]{2,1,0:T(8,128)(2,1)}, u32[]{:S(2)}, u32[]{:S(2)}) collective-permute-start(bf16[16,512,128]{2,1,0:T(8,128)(2,1)S(1)} %all_to_all.22), channel_id=1, source_target_pairs={{0,1},{1,0},{2,3},{3,2},{4,5},{5,4},{6,7},{7,6},{8,9},{9,8},{10,11... | collective-permute-start | bytes 6291464 | tf_op jit(solution)/shard_map/keys_values/ppermute | solution.py:172
  92.7 0.1 pad_add_fusion.place_ref
  92.8 3.8 %collective-permute-done = bf16[16,512,128]{2,1,0:T(8,128)(2,1)} collective-permute-done((bf16[16,512,128]{2,1,0:T(8,128)(2,1)S(1)}, bf16[16,512,128]{2,1,0:T(8,128)(2,1)}, u32[]{:S(2)}, u32[]{:S(2)}) %collective-permute-start) | collective-permute-done | bytes 2097184 | tf_op jit(solution)/shard_map/keys_values/ppermute | solution.py:172
  96.6 16.1 %attend.1 = bf16[4,2,2,32,640]{4,3,2,1,0:T(8,128)(2,1)S(1)} custom-call(s32[4]{0:T(128)S(1)} %pad_add_fusion.place_ref, bf16[4,2,2,32,640]{4,3,2,1,0:T(8,128)(2,1)S(1)} %bitcast.22, bf16[4,4,2,4,2,2,16,128]{7,6,5,4,3,2,1,0:T(8,128)(2,1)S(1)} %bitcast.21, bf16[4,4,2,4,2,2,16,128]{7,6,5,4,3,2,1,0:T(8,128)(2,1)} %bitcast.16.kv1_ref), custom_call_target="tpu_custom_call" | custom-call | tf_op jit(solution)/shard_map/attend/pallas_call | solution.py:117
  112.7 15.7 %all_to_all.23 = bf16[16,32,640]{2,1,0:T(8,128)(2,1)} all-to-all(bf16[16,32,640]{2,1,0:T(8,128)(2,1)S(1)} %bitcast.23), channel_id=1, replica_groups=mesh['xl'=2,'zh'=2,'zm'=2,'zl'=2,'yh'=2,'ym'=2,'yl'=2,'xh'=2,'co'=2] {'x..., dimensions={0} | all-to-all | bytes 1310720 | tf_op jit(solution)/shard_map/to_owners/all_to_all | solution.py:180
  128.5 2.4 %finish.1 = bf16[32,4096]{1,0:T(8,128)(2,1)} custom-call(bf16[4,2,2,32,640]{4,3,2,1,0:T(8,128)(2,1)} %bitcast.24), custom_call_target="tpu_custom_call" | custom-call | tf_op jit(solution)/shard_map/finish/pallas_call | solution.py:147
  (9 shorter events, 0.2 us)
Async XLA Ops:
  88.3 8.3 %collective-permute-start = (bf16[16,512,128]{2,1,0:T(8,128)(2,1)S(1)}, bf16[16,512,128]{2,1,0:T(8,128)(2,1)}, u32[]{:S(2)}, u32[]{:S(2)}) collective-permute-start(bf16[16,512,128]{2,1,0:T(8,128)(2,1)S(1)} %all_to_all.22), channel_id=1, source_target_pairs={{0,1},{1,0},{2,3},{3,2},{4,5},{5,4},{6,7},{7,6},{8,9},{9,8},{10,11... | collective-permute-start | bytes 6291464 | tf_op jit(solution)/shard_map/keys_values/ppermute | solution.py:172

commit v3 on v2

--- a/solution.py
+++ b/solution.py
@@ -21,7 +21,7 @@
 RANGES = 32
 ARG_SCALE = 1.0 / 600.0
 EXP_SCALE = 50.0 * math.log2(math.e)
-STEP = 8
+STEP = 16
 ROWS = 512
 
 bf16 = jnp.bfloat16
@@ -72,7 +72,7 @@
                 if t + 1 < count:
                     ahead = scores(t0 + t + 1)
                 w = jnp.exp2(jnp.tanh(s * ARG_SCALE) * EXP_SCALE)
-                if masked:
+                if masked and t >= count - 2:
                     r = lax.broadcasted_iota(jnp.int32, (ROWS, 1), 0)
                     r16 = ((r // 64) % 2) * 8 + w_own * 2 + (r // 32) % 2
                     r16 = jnp.where(e == 1, 15 - r16, r16)
@@ -87,13 +87,12 @@
             run(i * STEP, STEP, False)
             return c
 
-        def short(i, c):
-            run(first // STEP * STEP + i * 2, 2, False)
-            return c
-
         lax.fori_loop(0, first // STEP, long, 0)
-        lax.fori_loop(0, first % STEP // 2, short, 0)
-        run(first, 2, True)
+        rest = first % STEP
+        for count in range(0, STEP, 2):
+            @pl.when(rest == count)
+            def _(count=count):
+                run(first - count, count + 2, True)
 
         lane = lax.broadcasted_iota(jnp.int32, (128, HD), 1) // 16
         packed = jnp.zeros((128, HD), f32)
@@ -130,25 +129,24 @@
 
 
 def finish_kernel(x_ref, out_ref):
-    for xh in range(2):
-        for zz in range(4):
-            totals = x_ref[zz, 0, xh, :, WIDE:].astype(f32) + x_ref[zz, 1, xh, :, WIDE:].astype(f32)
-            for g in range(GROUP):
-                cols = slice(g * HD, (g + 1) * HD)
-                mixed = x_ref[zz, 0, xh, :, cols].astype(f32) + x_ref[zz, 1, xh, :, cols].astype(f32)
-                at = 32 * g
-                total = totals[:, at : at + 1] + totals[:, at + 16 : at + 17]
-                first = (xh * 4 + zz) * WIDE + g * HD
-                out_ref[:, first : first + HD] = (mixed / total).astype(bf16)
+    for zz in range(4):
+        totals = x_ref[zz, 0, 0, :, WIDE:].astype(f32) + x_ref[zz, 1, 0, :, WIDE:].astype(f32)
+        for g in range(GROUP):
+            cols = slice(g * HD, (g + 1) * HD)
+            mixed = x_ref[zz, 0, 0, :, cols].astype(f32) + x_ref[zz, 1, 0, :, cols].astype(f32)
+            at = 32 * g
+            total = totals[:, at : at + 1] + totals[:, at + 16 : at + 17]
+            first = zz * WIDE + g * HD
+            out_ref[:, first : first + HD] = (mixed / total).astype(bf16)
 
 
 def finish(x):
-    vmem = pl.BlockSpec(memory_space=pltpu.VMEM)
     return pl.pallas_call(
         finish_kernel,
+        grid=(2,),
         out_shape=jax.ShapeDtypeStruct((32, 8 * WIDE), bf16),
-        in_specs=[vmem],
-        out_specs=vmem,
+        in_specs=[pl.BlockSpec((4, 2, 1, 32, WIDE + HD), lambda xh: (0, 0, xh, 0, 0))],
+        out_specs=pl.BlockSpec((32, 4 * WIDE), lambda xh: (0, xh)),
         name="finish",
     )(x)
 

time: 131 us -> 129 us (0.985)
  Pallas kernels: 18.5 us -> 16.1 us
    pallas_call x1, Pallas kernels: 16.1 us -> 14 us  [attend(): pl.pallas_call(attend_kernel, out_shape=jax.ShapeDtypeStruct(q.shape, bf1...]
where the time goes in v3:
time: 129 us
  blocking collectives  102 us (79%)
  Pallas kernels  16.1 us (12%)
  starting transfers between devices  4.38 us (3%)
  waiting for transfers between devices  3.81 us (3%)
    all_to_all x1, blocking collectives, body(): kv0 = lax.all_to_all(spread, KEY_GROUP, 0, 0)  62.5 us
    all_to_all x1, blocking collectives, body(): lax.all_to_all(mixed.reshape(16, 32, WIDE + HD), QUERY_GROUP + ('xh',), 0...  15.7 us
    pallas_call x1, Pallas kernels, attend(): pl.pallas_call(attend_kernel, out_shape=jax.ShapeDtypeStruct(q.shape, bf1...  14 us
    all_to_all x1, blocking collectives, body(): got = lax.all_to_all(sent, QUERY_GROUP, 0, 0)  13.3 us
    all_to_all x1, blocking collectives, body(): heads = lax.all_to_all(mine, 'co', 0, 0)  10.6 us
    ppermute x1, starting transfers between devices, body(): kv1 = lax.ppermute(kv0, 'co', [(0, 1), (1, 0)])  4.38 us
    ppermute x1, waiting for transfers between devices, body(): kv1 = lax.ppermute(kv0, 'co', [(0, 1), (1, 0)])  3.81 us
  transfers between devices with their start and end apart: 1, of which 1 were waited for; matrix products, arithmetic and copies ran while one was open for 0% of the time, Pallas kernels for 0%

profile of v3, /device:TPU:1, one launch (start us, length us, event | category | flops | bytes accessed | tf_op | source)
XLA Modules:
  0.0 128.5 jit_solution(12547585246673572761)
XLA Ops:
  0.0 1.1 pad_maximum_fusion.1
  1.1 10.6 %all_to_all.20 = bf16[2,64,1536]{2,1,0:T(8,128)(2,1)S(1)} all-to-all(bf16[2,64,1536]{2,1,0:T(8,128)(2,1)S(1)} %bitcast.26), channel_id=1, replica_groups=mesh['xl'=2,'zh'=2,'zm'=2,'zl'=2,'yh'=2,'ym'=2,'yl'=2,'xh'=2,'co'=2] {'co'}, dimensions={0} | all-to-all | bytes 786432 | tf_op jit(solution)/shard_map/to_cores/all_to_all | solution.py:158
  11.7 0.2 reshape.42
  12.0 0.1 pad_maximum_fusion
  12.1 13.3 %all_to_all.21 = bf16[8,64,640]{2,1,0:T(8,128)(2,1)S(1)} all-to-all(bf16[8,64,640]{2,1,0:T(8,128)(2,1)S(1)} %pad_maximum_fusion), channel_id=1, replica_groups=mesh['xl'=2,'zh'=2,'zm'=2,'zl'=2,'yh'=2,'ym'=2,'yl'=2,'xh'=2,'co'=2] {'x..., dimensions={0} | all-to-all | bytes 1310720 | tf_op jit(solution)/shard_map/to_heads/all_to_all | solution.py:165
  25.5 0.4 broadcast_in_dim.16
  25.9 62.5 %all_to_all.22 = bf16[16,512,128]{2,1,0:T(8,128)(2,1)S(1)} all-to-all(bf16[16,512,128]{2,1,0:T(8,128)(2,1)S(1)} %broadcast_in_dim.16), channel_id=1, replica_groups=mesh['xl'=2,'zh'=2,'zm'=2,'zl'=2,'yh'=2,'ym'=2,'yl'=2,'xh'=2,'co'=2] {'z..., dimensions={0} | all-to-all | bytes 4194304 | tf_op jit(solution)/shard_map/keys_values/all_to_all | solution.py:169
  88.3 4.4 %collective-permute-start = (bf16[16,512,128]{2,1,0:T(8,128)(2,1)S(1)}, bf16[16,512,128]{2,1,0:T(8,128)(2,1)}, u32[]{:S(2)}, u32[]{:S(2)}) collective-permute-start(bf16[16,512,128]{2,1,0:T(8,128)(2,1)S(1)} %all_to_all.22), channel_id=1, source_target_pairs={{0,1},{1,0},{2,3},{3,2},{4,5},{5,4},{6,7},{7,6},{8,9},{9,8},{10,11... | collective-permute-start | bytes 6291464 | tf_op jit(solution)/shard_map/keys_values/ppermute | solution.py:170
  92.7 0.1 pad_add_fusion.place_ref
  92.8 3.8 %collective-permute-done = bf16[16,512,128]{2,1,0:T(8,128)(2,1)} collective-permute-done((bf16[16,512,128]{2,1,0:T(8,128)(2,1)S(1)}, bf16[16,512,128]{2,1,0:T(8,128)(2,1)}, u32[]{:S(2)}, u32[]{:S(2)}) %collective-permute-start) | collective-permute-done | bytes 2097184 | tf_op jit(solution)/shard_map/keys_values/ppermute | solution.py:170
  96.6 14.0 %attend.1 = bf16[4,2,2,32,640]{4,3,2,1,0:T(8,128)(2,1)S(1)} custom-call(s32[4]{0:T(128)S(1)} %pad_add_fusion.place_ref, bf16[4,2,2,32,640]{4,3,2,1,0:T(8,128)(2,1)S(1)} %bitcast.22, bf16[4,4,2,4,2,2,16,128]{7,6,5,4,3,2,1,0:T(8,128)(2,1)S(1)} %bitcast.21, bf16[4,4,2,4,2,2,16,128]{7,6,5,4,3,2,1,0:T(8,128)(2,1)} %bitcast.16.kv1_ref), custom_call_target="tpu_custom_call" | custom-call | tf_op jit(solution)/shard_map/attend/pallas_call | solution.py:116
  110.6 15.7 %all_to_all.23 = bf16[16,32,640]{2,1,0:T(8,128)(2,1)} all-to-all(bf16[16,32,640]{2,1,0:T(8,128)(2,1)S(1)} %bitcast.23), channel_id=1, replica_groups=mesh['xl'=2,'zh'=2,'zm'=2,'zl'=2,'yh'=2,'ym'=2,'yl'=2,'xh'=2,'co'=2] {'x..., dimensions={0} | all-to-all | bytes 1310720 | tf_op jit(solution)/shard_map/to_owners/all_to_all | solution.py:178
  126.4 2.1 %finish.1 = bf16[32,4096]{1,0:T(8,128)(2,1)} custom-call(bf16[4,2,2,32,640]{4,3,2,1,0:T(8,128)(2,1)} %bitcast.24), custom_call_target="tpu_custom_call" | custom-call | tf_op jit(solution)/shard_map/finish/pallas_call | solution.py:144
  (9 shorter events, 0.2 us)
Async XLA Ops:
  88.3 8.3 %collective-permute-start = (bf16[16,512,128]{2,1,0:T(8,128)(2,1)S(1)}, bf16[16,512,128]{2,1,0:T(8,128)(2,1)}, u32[]{:S(2)}, u32[]{:S(2)}) collective-permute-start(bf16[16,512,128]{2,1,0:T(8,128)(2,1)S(1)} %all_to_all.22), channel_id=1, source_target_pairs={{0,1},{1,0},{2,3},{3,2},{4,5},{5,4},{6,7},{7,6},{8,9},{9,8},{10,11... | collective-permute-start | bytes 6291464 | tf_op jit(solution)/shard_map/keys_values/ppermute | solution.py:170

commit v4 on v3

--- a/solution.py
+++ b/solution.py
@@ -155,7 +155,11 @@
     with jax.named_scope("to_cores"):
         mine = jnp.concatenate([queries, keys, values], axis=1).reshape(2, 2, 32, 1536)
         mine = mine.transpose(1, 0, 2, 3).reshape(2, 64, 1536)
-        heads = lax.all_to_all(mine, "co", 0, 0)
+        core = lax.axis_index("co")
+        kept = lax.dynamic_index_in_dim(mine, core, 0, keepdims=False)
+        given = lax.dynamic_index_in_dim(mine, 1 - core, 0, keepdims=False)
+        taken = lax.ppermute(given, "co", [(0, 1), (1, 0)])
+        heads = jnp.stack([jnp.where(core == 0, kept, taken), jnp.where(core == 0, taken, kept)])
     with jax.named_scope("to_heads"):
         q = heads[:, :, :1024].reshape(2, 64, 2, WIDE).transpose(0, 2, 1, 3)
         kv = heads[:, :, 1024:].reshape(2, 2, 2, 16, 2, 2, HD)

time: 129 us -> 128 us (level)
  blocking collectives: 102 us -> 91.5 us
  starting transfers between devices: 4.38 us -> 13.2 us
    all_to_all x1 -> x0, blocking collectives: 10.6 us -> none  [body(): heads = lax.all_to_all(mine, 'co', 0, 0)]
    ppermute x0 -> x1, starting transfers between devices: none -> 8.79 us  [body(): taken = lax.ppermute(given, 'co', [(0, 1), (1, 0)])]
  transfers between devices with their start and end apart: 1 -> 2, of which waited for: 1 -> 2; matrix products, arithmetic and copies ran while one was open for 0% -> 0% of each run, Pallas kernels for 0% -> 0%
where the time goes in v4:
time: 128 us
  blocking collectives  91.5 us (71%)
  Pallas kernels  16.1 us (13%)
  starting transfers between devices  13.2 us (10%)
  waiting for transfers between devices  4.85 us (4%)
    all_to_all x1, blocking collectives, body(): kv0 = lax.all_to_all(spread, KEY_GROUP, 0, 0)  62.5 us
    all_to_all x1, blocking collectives, body(): lax.all_to_all(mixed.reshape(16, 32, WIDE + HD), QUERY_GROUP + ('xh',), 0...  15.7 us
    pallas_call x1, Pallas kernels, attend(): pl.pallas_call(attend_kernel, out_shape=jax.ShapeDtypeStruct(q.shape, bf1...  14 us
    all_to_all x1, blocking collectives, body(): got = lax.all_to_all(sent, QUERY_GROUP, 0, 0)  13.3 us
    ppermute x1, starting transfers between devices, body(): taken = lax.ppermute(given, 'co', [(0, 1), (1, 0)])  8.79 us
    ppermute x1, starting transfers between devices, body(): kv1 = lax.ppermute(kv0, 'co', [(0, 1), (1, 0)])  4.38 us
    ppermute x1, waiting for transfers between devices, body(): kv1 = lax.ppermute(kv0, 'co', [(0, 1), (1, 0)])  3.81 us
  transfers between devices with their start and end apart: 2, of which 2 were waited for; matrix products, arithmetic and copies ran while one was open for 0% of the time, Pallas kernels for 0%

profile of v4, /device:TPU:1, one launch (start us, length us, event | category | flops | bytes accessed | tf_op | source)
XLA Modules:
  0.0 127.8 jit_solution(15191836887843014412)
XLA Ops:
  0.0 1.1 pad_maximum_fusion.1
  1.1 8.8 %collective-permute-start = (bf16[64,1536]{1,0:T(8,128)(2,1)S(1)}, bf16[64,1536]{1,0:T(8,128)(2,1)S(1)}, u32[]{:S(2)}, u32[]{:S(2)}) collective-permute-start(bf16[64,1536]{1,0:T(8,128)(2,1)S(1)} %dynamic-slice_bitcast_fusion), channel_id=1, source_target_pairs={{0,1},{1,0},{2,3},{3,2},{4,5},{5,4},{6,7},{7,6},{8,9},{9,8},{10,11... | collective-permute-start | bytes 589832 | tf_op jit(solution)/shard_map/to_cores/ppermute | solution.py:161
  9.9 1.0 collective-permute-done
  11.1 0.2 reshape.42
  11.4 0.1 pad_maximum_fusion
  11.5 13.3 %all_to_all.15 = bf16[8,64,640]{2,1,0:T(8,128)(2,1)S(1)} all-to-all(bf16[8,64,640]{2,1,0:T(8,128)(2,1)S(1)} %pad_maximum_fusion), channel_id=1, replica_groups=mesh['xl'=2,'zh'=2,'zm'=2,'zl'=2,'yh'=2,'ym'=2,'yl'=2,'xh'=2,'co'=2] {'x..., dimensions={0} | all-to-all | bytes 1310720 | tf_op jit(solution)/shard_map/to_heads/all_to_all | solution.py:169
  24.8 0.4 broadcast_in_dim.16
  25.2 62.5 %all_to_all.16 = bf16[16,512,128]{2,1,0:T(8,128)(2,1)S(1)} all-to-all(bf16[16,512,128]{2,1,0:T(8,128)(2,1)S(1)} %broadcast_in_dim.16), channel_id=1, replica_groups=mesh['xl'=2,'zh'=2,'zm'=2,'zl'=2,'yh'=2,'ym'=2,'yl'=2,'xh'=2,'co'=2] {'z..., dimensions={0} | all-to-all | bytes 4194304 | tf_op jit(solution)/shard_map/keys_values/all_to_all | solution.py:173
  87.7 4.4 %collective-permute-start.1 = (bf16[16,512,128]{2,1,0:T(8,128)(2,1)S(1)}, bf16[16,512,128]{2,1,0:T(8,128)(2,1)}, u32[]{:S(2)}, u32[]{:S(2)}) collective-permute-start(bf16[16,512,128]{2,1,0:T(8,128)(2,1)S(1)} %all_to_all.16), channel_id=1, source_target_pairs={{0,1},{1,0},{2,3},{3,2},{4,5},{5,4},{6,7},{7,6},{8,9},{9,8},{10,11... | collective-permute-start | bytes 6291464 | tf_op jit(solution)/shard_map/keys_values/ppermute | solution.py:174
  92.1 0.1 pad_add_fusion.place_ref
  92.2 3.8 %collective-permute-done.1 = bf16[16,512,128]{2,1,0:T(8,128)(2,1)} collective-permute-done((bf16[16,512,128]{2,1,0:T(8,128)(2,1)S(1)}, bf16[16,512,128]{2,1,0:T(8,128)(2,1)}, u32[]{:S(2)}, u32[]{:S(2)}) %collective-permute-start.1) | collective-permute-done | bytes 2097184 | tf_op jit(solution)/shard_map/keys_values/ppermute | solution.py:174
  96.0 14.0 %attend.1 = bf16[4,2,2,32,640]{4,3,2,1,0:T(8,128)(2,1)S(1)} custom-call(s32[4]{0:T(128)S(1)} %pad_add_fusion.place_ref, bf16[4,2,2,32,640]{4,3,2,1,0:T(8,128)(2,1)S(1)} %bitcast.35, bf16[4,4,2,4,2,2,16,128]{7,6,5,4,3,2,1,0:T(8,128)(2,1)S(1)} %bitcast.34, bf16[4,4,2,4,2,2,16,128]{7,6,5,4,3,2,1,0:T(8,128)(2,1)} %bitcast.20.kv1_ref), custom_call_target="tpu_custom_call" | custom-call | tf_op jit(solution)/shard_map/attend/pallas_call | solution.py:116
  110.0 15.7 %all_to_all.17 = bf16[16,32,640]{2,1,0:T(8,128)(2,1)} all-to-all(bf16[16,32,640]{2,1,0:T(8,128)(2,1)S(1)} %bitcast.36), channel_id=1, replica_groups=mesh['xl'=2,'zh'=2,'zm'=2,'zl'=2,'yh'=2,'ym'=2,'yl'=2,'xh'=2,'co'=2] {'x..., dimensions={0} | all-to-all | bytes 1310720 | tf_op jit(solution)/shard_map/to_owners/all_to_all | solution.py:182
  125.7 2.1 %finish.1 = bf16[32,4096]{1,0:T(8,128)(2,1)} custom-call(bf16[4,2,2,32,640]{4,3,2,1,0:T(8,128)(2,1)} %bitcast.37), custom_call_target="tpu_custom_call" | custom-call | tf_op jit(solution)/shard_map/finish/pallas_call | solution.py:144
  (11 shorter events, 0.3 us)
Async XLA Ops:
  1.1 9.8 %collective-permute-start = (bf16[64,1536]{1,0:T(8,128)(2,1)S(1)}, bf16[64,1536]{1,0:T(8,128)(2,1)S(1)}, u32[]{:S(2)}, u32[]{:S(2)}) collective-permute-start(bf16[64,1536]{1,0:T(8,128)(2,1)S(1)} %dynamic-slice_bitcast_fusion), channel_id=1, source_target_pairs={{0,1},{1,0},{2,3},{3,2},{4,5},{5,4},{6,7},{7,6},{8,9},{9,8},{10,11... | collective-permute-start | bytes 589832 | tf_op jit(solution)/shard_map/to_cores/ppermute | solution.py:161
  87.7 8.3 %collective-permute-start.1 = (bf16[16,512,128]{2,1,0:T(8,128)(2,1)S(1)}, bf16[16,512,128]{2,1,0:T(8,128)(2,1)}, u32[]{:S(2)}, u32[]{:S(2)}) collective-permute-start(bf16[16,512,128]{2,1,0:T(8,128)(2,1)S(1)} %all_to_all.16), channel_id=1, source_target_pairs={{0,1},{1,0},{2,3},{3,2},{4,5},{5,4},{6,7},{7,6},{8,9},{9,8},{10,11... | collective-permute-start | bytes 6291464 | tf_op jit(solution)/shard_map/keys_values/ppermute | solution.py:174

commit v5 on v4

--- a/solution.py
+++ b/solution.py
@@ -153,11 +153,14 @@
 
 def body(queries, keys, values):
     with jax.named_scope("to_cores"):
-        mine = jnp.concatenate([queries, keys, values], axis=1).reshape(2, 2, 32, 1536)
-        mine = mine.transpose(1, 0, 2, 3).reshape(2, 64, 1536)
         core = lax.axis_index("co")
-        kept = lax.dynamic_index_in_dim(mine, core, 0, keepdims=False)
-        given = lax.dynamic_index_in_dim(mine, 1 - core, 0, keepdims=False)
+
+        def rows_of(one):
+            parts = [x.reshape(2, 2, 32, x.shape[1]) for x in (queries, keys, values)]
+            parts = [lax.dynamic_index_in_dim(x, one, 1, keepdims=False) for x in parts]
+            return jnp.concatenate(parts, axis=-1).reshape(64, 1536)
+
+        given, kept = rows_of(1 - core), rows_of(core)
         taken = lax.ppermute(given, "co", [(0, 1), (1, 0)])
         heads = jnp.stack([jnp.where(core == 0, kept, taken), jnp.where(core == 0, taken, kept)])
     with jax.named_scope("to_heads"):

time: 128 us -> 129 us (level)
  local copies, waits for them, and re-layouts: 0.79 us -> 2.56 us
    dynamic_slice x0 -> x2, local copies, waits for them, and re-layouts: none -> 1.82 us  [rows_of(): parts = [lax.dynamic_index_in_dim(x, one, 1, keepdims=False) for x in parts]]
where the time goes in v5:
time: 129 us
  blocking collectives  91.5 us (71%)
  Pallas kernels  16.1 us (12%)
  starting transfers between devices  13.2 us (10%)
  waiting for transfers between devices  4.85 us (4%)
  local copies, waits for them, and re-layouts  2.56 us (2%)
    all_to_all x1, blocking collectives, body(): kv0 = lax.all_to_all(spread, KEY_GROUP, 0, 0)  62.5 us
    all_to_all x1, blocking collectives, body(): lax.all_to_all(mixed.reshape(16, 32, WIDE + HD), QUERY_GROUP + ('xh',), 0...  15.7 us
    pallas_call x1, Pallas kernels, attend(): pl.pallas_call(attend_kernel, out_shape=jax.ShapeDtypeStruct(q.shape, bf1...  14 us
    all_to_all x1, blocking collectives, body(): got = lax.all_to_all(sent, QUERY_GROUP, 0, 0)  13.3 us
    ppermute x1, starting transfers between devices, body(): taken = lax.ppermute(given, 'co', [(0, 1), (1, 0)])  8.79 us
    ppermute x1, starting transfers between devices, body(): kv1 = lax.ppermute(kv0, 'co', [(0, 1), (1, 0)])  4.38 us
    ppermute x1, waiting for transfers between devices, body(): kv1 = lax.ppermute(kv0, 'co', [(0, 1), (1, 0)])  3.81 us
  transfers between devices with their start and end apart: 2, of which 2 were waited for; matrix products, arithmetic and copies ran while one was open for 0% of the time, Pallas kernels for 0%

profile of v5, /device:TPU:1, one launch (start us, length us, event | category | flops | bytes accessed | tf_op | source)
XLA Modules:
  0.0 128.6 jit_solution(6425047053622250244)
XLA Ops:
  0.0 1.0 constant_dynamic-slice_fusion.5
  1.0 0.8 constant_dynamic-slice_fusion.3
  1.8 8.8 %collective-permute-start = (bf16[64,1536]{1,0:T(8,128)(2,1)S(1)}, bf16[64,1536]{1,0:T(8,128)(2,1)S(1)}, u32[]{:S(2)}, u32[]{:S(2)}) collective-permute-start(bf16[64,1536]{1,0:T(8,128)(2,1)S(1)} %pad_maximum_fusion.2), channel_id=1, source_target_pairs={{0,1},{1,0},{2,3},{3,2},{4,5},{5,4},{6,7},{7,6},{8,9},{9,8},{10,11... | collective-permute-start | bytes 589832 | tf_op jit(solution)/shard_map/to_cores/ppermute | solution.py:164
  10.6 1.0 collective-permute-done
  11.7 0.1 select_bitcast_fusion.1
  11.8 0.2 reshape.63
  12.2 0.1 pad_maximum_fusion
  12.2 13.3 %all_to_all.15 = bf16[8,64,640]{2,1,0:T(8,128)(2,1)S(1)} all-to-all(bf16[8,64,640]{2,1,0:T(8,128)(2,1)S(1)} %pad_maximum_fusion), channel_id=1, replica_groups=mesh['xl'=2,'zh'=2,'zm'=2,'zl'=2,'yh'=2,'ym'=2,'yl'=2,'xh'=2,'co'=2] {'x..., dimensions={0} | all-to-all | bytes 1310720 | tf_op jit(solution)/shard_map/to_heads/all_to_all | solution.py:172
  25.6 0.4 broadcast_in_dim.16
  26.0 62.5 %all_to_all.16 = bf16[16,512,128]{2,1,0:T(8,128)(2,1)S(1)} all-to-all(bf16[16,512,128]{2,1,0:T(8,128)(2,1)S(1)} %broadcast_in_dim.16), channel_id=1, replica_groups=mesh['xl'=2,'zh'=2,'zm'=2,'zl'=2,'yh'=2,'ym'=2,'yl'=2,'xh'=2,'co'=2] {'z..., dimensions={0} | all-to-all | bytes 4194304 | tf_op jit(solution)/shard_map/keys_values/all_to_all | solution.py:176
  88.5 4.4 %collective-permute-start.1 = (bf16[16,512,128]{2,1,0:T(8,128)(2,1)S(1)}, bf16[16,512,128]{2,1,0:T(8,128)(2,1)}, u32[]{:S(2)}, u32[]{:S(2)}) collective-permute-start(bf16[16,512,128]{2,1,0:T(8,128)(2,1)S(1)} %all_to_all.16), channel_id=1, source_target_pairs={{0,1},{1,0},{2,3},{3,2},{4,5},{5,4},{6,7},{7,6},{8,9},{9,8},{10,11... | collective-permute-start | bytes 6291464 | tf_op jit(solution)/shard_map/keys_values/ppermute | solution.py:177
  92.8 0.1 pad_add_fusion.place_ref
  92.9 3.8 %collective-permute-done.1 = bf16[16,512,128]{2,1,0:T(8,128)(2,1)} collective-permute-done((bf16[16,512,128]{2,1,0:T(8,128)(2,1)S(1)}, bf16[16,512,128]{2,1,0:T(8,128)(2,1)}, u32[]{:S(2)}, u32[]{:S(2)}) %collective-permute-start.1) | collective-permute-done | bytes 2097184 | tf_op jit(solution)/shard_map/keys_values/ppermute | solution.py:177
  96.7 14.0 %attend.1 = bf16[4,2,2,32,640]{4,3,2,1,0:T(8,128)(2,1)S(1)} custom-call(s32[4]{0:T(128)S(1)} %pad_add_fusion.place_ref, bf16[4,2,2,32,640]{4,3,2,1,0:T(8,128)(2,1)S(1)} %bitcast.31, bf16[4,4,2,4,2,2,16,128]{7,6,5,4,3,2,1,0:T(8,128)(2,1)S(1)} %bitcast.30, bf16[4,4,2,4,2,2,16,128]{7,6,5,4,3,2,1,0:T(8,128)(2,1)} %bitcast.24.kv1_ref), custom_call_target="tpu_custom_call" | custom-call | tf_op jit(solution)/shard_map/attend/pallas_call | solution.py:116
  110.8 15.7 %all_to_all.17 = bf16[16,32,640]{2,1,0:T(8,128)(2,1)} all-to-all(bf16[16,32,640]{2,1,0:T(8,128)(2,1)S(1)} %bitcast.32), channel_id=1, replica_groups=mesh['xl'=2,'zh'=2,'zm'=2,'zl'=2,'yh'=2,'ym'=2,'yl'=2,'xh'=2,'co'=2] {'x..., dimensions={0} | all-to-all | bytes 1310720 | tf_op jit(solution)/shard_map/to_owners/all_to_all | solution.py:185
  126.5 2.1 %finish.1 = bf16[32,4096]{1,0:T(8,128)(2,1)} custom-call(bf16[4,2,2,32,640]{4,3,2,1,0:T(8,128)(2,1)} %bitcast.33), custom_call_target="tpu_custom_call" | custom-call | tf_op jit(solution)/shard_map/finish/pallas_call | solution.py:144
  (9 shorter events, 0.2 us)
Async XLA Ops:
  1.8 9.8 %collective-permute-start = (bf16[64,1536]{1,0:T(8,128)(2,1)S(1)}, bf16[64,1536]{1,0:T(8,128)(2,1)S(1)}, u32[]{:S(2)}, u32[]{:S(2)}) collective-permute-start(bf16[64,1536]{1,0:T(8,128)(2,1)S(1)} %pad_maximum_fusion.2), channel_id=1, source_target_pairs={{0,1},{1,0},{2,3},{3,2},{4,5},{5,4},{6,7},{7,6},{8,9},{9,8},{10,11... | collective-permute-start | bytes 589832 | tf_op jit(solution)/shard_map/to_cores/ppermute | solution.py:164
  88.5 8.3 %collective-permute-start.1 = (bf16[16,512,128]{2,1,0:T(8,128)(2,1)S(1)}, bf16[16,512,128]{2,1,0:T(8,128)(2,1)}, u32[]{:S(2)}, u32[]{:S(2)}) collective-permute-start(bf16[16,512,128]{2,1,0:T(8,128)(2,1)S(1)} %all_to_all.16), channel_id=1, source_target_pairs={{0,1},{1,0},{2,3},{3,2},{4,5},{5,4},{6,7},{7,6},{8,9},{9,8},{10,11... | collective-permute-start | bytes 6291464 | tf_op jit(solution)/shard_map/keys_values/ppermute | solution.py:177
